TPU v7x, 512 devices: a whole 4x4x16 slice. The times are simulated.
512 devices in a mesh: ctx: 64 (over z_hi, x, y, core), head: 8 (over z_lo).
Axes of the slice: x: 4, y: 4, z: 16 (z_hi: 2, z_lo: 8; z = z_hi * 8 + z_lo), core: 2. Of those that a mesh axis runs over, the one named last changes fastest.
Arguments:
- query_rows: bfloat16 [32768, 4096], P('ctx', 'head'), may hold values from -32 to 32
- key_rows: bfloat16 [32768, 1024], P('ctx', 'head'), may hold values from -32 to 32
- value_rows: bfloat16 [32768, 1024], P('ctx', 'head'), may hold values from -6 to 6
- out_weight: bfloat16 [4096, 4096], P('head', 'ctx'), may hold values from -0.71875 to 0.71875
Outputs:
- attended: bfloat16 [32768, 4096], P('ctx', 'head')
All inputs are finite; a program needn't handle non-finite values.
Results may differ from a plain program's by a relative error of at most 0.015.
Values may be sent and summed in bfloat16 or wider, within the bound.
A program may use at most 64 MiB of HBM per device.

v0:
```python
import jax
import jax.numpy as jnp
from jax import lax
from jax.sharding import PartitionSpec as P

HD = 128
BLOCK = 512


def from_partner(shard, axis, bit):
    return lax.ppermute(shard, axis, [(i, i ^ 1 << bit) for i in range(lax.axis_size(axis))])


def combine(state, update):
    peak_old, total_old, output_old = state
    peak_new, total_new, output_new = update
    top = jnp.maximum(peak_old, peak_new)
    scale_old = jnp.exp(peak_old - top)
    scale_new = jnp.exp(peak_new - top)
    total = scale_old * total_old + scale_new * total_new
    output = scale_old[..., None] * output_old + scale_new[..., None] * output_new
    return (top, total, output)


def shards(query_rows, key_rows, value_rows, out_weight):
    tok_rows, query_cols = query_rows.shape
    block_count = tok_rows // BLOCK
    heads_kv = key_rows.shape[1] // HD
    heads_query = query_cols // HD
    group = heads_query // heads_kv
    queries = query_rows.reshape(block_count, BLOCK, heads_kv, group, HD)
    stacked = jnp.stack(
        [
            key_rows.reshape(block_count, BLOCK, heads_kv, HD),
            value_rows.reshape(block_count, BLOCK, heads_kv, HD),
        ]
    )
    factor = HD ** (-0.5)

    def block_stats(pair):
        scores = (
            jnp.einsum("bqgrd,bkgd->bgrqk", queries, pair[0], preferred_element_type=jnp.float32)
            * factor
        )
        peak = jnp.max(scores, axis=-1)
        weights = jnp.exp(scores - peak[..., None])
        total = jnp.sum(weights, axis=-1)
        probs = weights.astype(jnp.bfloat16)
        output = jnp.einsum("bgrqk,bkgd->bgrqd", probs, pair[1], preferred_element_type=jnp.float32)
        return (peak, total, output)

    state = block_stats(stacked)
    level_list = list(range(lax.axis_size("ctx").bit_length() - 1))
    for level in level_list:
        partner = from_partner(stacked, "ctx", level)
        state = combine(state, block_stats(partner))
    hidden = state[2] / state[1][..., None]
    hidden = hidden.transpose(0, 3, 1, 2, 4).reshape(tok_rows, query_cols).astype(jnp.bfloat16)
    terms = jnp.dot(
        hidden,
        lax.all_gather(out_weight, "ctx", axis=1, tiled=True),
        preferred_element_type=jnp.float32,
    )
    return lax.psum_scatter(terms.astype(jnp.bfloat16), "head", scatter_dimension=1, tiled=True)


def solution(mesh):
    placed = (P("ctx", "head"), P("ctx", "head"), P("ctx", "head"), P("head", "ctx"))
    return jax.shard_map(
        shards, mesh=mesh, in_specs=placed, out_specs=P("ctx", "head"), check_vma=False
    )
```

profile of v0, /device:TPU:1, one launch (start us, length us, event | category | flops | bytes accessed | tf_op | source)
XLA Modules:
  0.0 273.2 jit_solution(7072032613657819309)
XLA Ops:
  6.5 0.7 all-gather.2.cloned.1.call-update
  7.3 1.0 pad_maximum_fusion
  8.3 3.9 %collective-permute-start.3 = (bf16[2,1,512,1,128]{4,2,3,1,0:T(8,128)(2,1)S(1)}, bf16[2,1,512,1,128]{4,2,3,1,0:T(8,128)(2,1)S(1)}, u32[]{:S(2)}, u32[]{:S(2)}) collective-permute-start(bf16[2,1,512,1,128]{4,2,3,1,0:T(8,128)(2,1)S(1)} %pad_maximum_fusion), channel_id=1, source_target_pairs={{0,64},{8,72},{16,80},{24,88},{32,96},{40,104},{48,112},{56,120},{... | collective-permute-start | bytes 786440 | tf_op jit(solution)/shard_map/ppermute | solution.py:11
  12.3 4.8 %collective-permute-start.2 = (bf16[2,1,512,1,128]{4,2,3,1,0:T(8,128)(2,1)S(1)}, bf16[2,1,512,1,128]{4,2,3,1,0:T(8,128)(2,1)S(1)}, u32[]{:S(2)}, u32[]{:S(2)}) collective-permute-start(bf16[2,1,512,1,128]{4,2,3,1,0:T(8,128)(2,1)S(1)} %pad_maximum_fusion), channel_id=1, source_target_pairs={{0,32},{8,40},{16,48},{24,56},{32,0},{40,8},{48,16},{56,24},{64,96... | collective-permute-start | bytes 786440 | tf_op jit(solution)/shard_map/ppermute | solution.py:11
  17.1 2.3 collective-permute-start.1
  19.4 3.5 %collective-permute-start = (bf16[2,1,512,1,128]{4,2,3,1,0:T(8,128)(2,1)S(1)}, bf16[2,1,512,1,128]{4,2,3,1,0:T(8,128)(2,1)S(1)}, u32[]{:S(2)}, u32[]{:S(2)}) collective-permute-start(bf16[2,1,512,1,128]{4,2,3,1,0:T(8,128)(2,1)S(1)} %pad_maximum_fusion), channel_id=1, source_target_pairs={{0,8},{8,0},{16,24},{24,16},{32,40},{40,32},{48,56},{56,48},{64,72... | collective-permute-start | bytes 786440 | tf_op jit(solution)/shard_map/ppermute | solution.py:11
  22.9 4.3 %collective-permute-start.4 = (bf16[2,1,512,1,128]{4,2,3,1,0:T(8,128)(2,1)S(1)}, bf16[2,1,512,1,128]{4,2,3,1,0:T(8,128)(2,1)S(1)}, u32[]{:S(2)}, u32[]{:S(2)}) collective-permute-start(bf16[2,1,512,1,128]{4,2,3,1,0:T(8,128)(2,1)S(1)} %pad_maximum_fusion), channel_id=1, source_target_pairs={{0,128},{8,136},{16,144},{24,152},{32,160},{40,168},{48,176},{56,1... | collective-permute-start | bytes 786440 | tf_op jit(solution)/shard_map/ppermute | solution.py:11
  27.2 1.6 bitcast_reduce_fusion.6
  28.8 0.7 fusion.7
  29.6 15.4 %collective-permute-start.5 = (bf16[2,1,512,1,128]{4,2,3,1,0:T(8,128)(2,1)S(1)}, bf16[2,1,512,1,128]{4,2,3,1,0:T(8,128)(2,1)S(1)}, u32[]{:S(2)}, u32[]{:S(2)}) collective-permute-start(bf16[2,1,512,1,128]{4,2,3,1,0:T(8,128)(2,1)S(1)} %pad_maximum_fusion), channel_id=1, source_target_pairs={{0,256},{8,264},{16,272},{24,280},{32,288},{40,296},{48,304},{56,3... | collective-permute-start | bytes 786440 | tf_op jit(solution)/shard_map/ppermute | solution.py:11
  45.0 0.7 bitcast_reduce_fusion.4
  45.7 0.7 fusion.11
  46.5 0.7 bitcast_reduce_fusion.3
  47.2 0.7 fusion.13
  47.9 0.7 bitcast_reduce_fusion.2
  48.6 0.7 fusion.15
  49.3 0.7 bitcast_reduce_fusion.5
  50.1 0.7 fusion.9
  50.8 0.7 bitcast_reduce_fusion.1
  51.5 0.7 fusion.17
  52.2 4.7 %collective-permute-done.5 = bf16[2,1,512,1,128]{4,2,3,1,0:T(8,128)(2,1)S(1)} collective-permute-done((bf16[2,1,512,1,128]{4,2,3,1,0:T(8,128)(2,1)S(1)}, bf16[2,1,512,1,128]{4,2,3,1,0:T(8,128)(2,1)S(1)}, u32[]{:S(2)}, u32[]{:S(2)}) %collective-permute-start.5) | collective-permute-done | bytes 262176 | tf_op jit(solution)/shard_map/ppermute | solution.py:11
  56.9 0.7 bitcast_reduce_fusion
  58.5 0.9 fusion.56
  59.4 0.9 fusion.77
  60.3 0.9 fusion.80
  61.3 0.9 fusion.83
  62.2 1.1 fusion.86
  63.3 0.9 fusion.89
  64.3 1.7 fusion.113
  66.0 99.9 %all-gather.2.cloned.1.call-done = bf16[512,4096]{0,1:T(8,128)(2,1)} async-done(((bf16[512,64]{0,1:T(8,128)(2,1)}), bf16[512,4096]{0,1:T(8,128)(2,1)}) %all-gather.2.cloned.1.call-update) | async-done | bytes 4194320 | tf_op jit(solution)/shard_map/all_gather | solution.py:61
  165.8 6.6 %convolution_convert_fusion = bf16[512,4096]{1,0:T(8,128)(2,1)} fusion(bf16[512,512]{0,1:T(8,128)(2,1)S(1)} %bitcast.339, bf16[512,4096]{0,1:T(8,128)(2,1)} %all-gather.2.cloned.1.call-done), kind=kOutput, calls=%fused_computation | convolution fusion | flops 2149580800 | bytes 8912896 | tf_op jit(solution)/shard_map/dot_general | solution.py:59
  172.4 94.0 %reduce-scatter.2.cloned.1.call-done = bf16[512,512]{1,0:T(8,128)(2,1)} async-done(((bf16[512,4096]{1,0:T(8,128)(2,1)}), bf16[512,512]{1,0:T(8,128)(2,1)}) %reduce-scatter.2.cloned.1.call-update) | async-done | bytes 524304 | tf_op jit(solution)/shard_map/reduce_scatter | solution.py:64
  (15 shorter events, 0.9 us)
Async XLA Ops:
  6.5 20.7 %copy-start = (bf16[512,512]{1,0:T(8,128)(2,1)S(1)}, bf16[512,512]{1,0:T(8,128)(2,1)}, u32[]{:S(2)}) copy-start(bf16[512,512]{1,0:T(8,128)(2,1)} %param.4) | copy-start | bytes 1572868
  6.5 159.3 %all-gather.2.cloned.1.call-start = ((), (), s32[]{:S(2)}) async-start(), calls=%async_computation.1 | async-start | bytes 4259840 | tf_op jit(solution)/shard_map/all_gather | solution.py:61
  7.3 259.1 %reduce-scatter.2.cloned.1.call-start = ((), (), s32[]{:S(2)}) async-start(), calls=%async_computation.2 | async-start | bytes 4718592 | tf_op jit(solution)/shard_map/reduce_scatter | solution.py:64
  8.3 39.6 %collective-permute-start.3 = (bf16[2,1,512,1,128]{4,2,3,1,0:T(8,128)(2,1)S(1)}, bf16[2,1,512,1,128]{4,2,3,1,0:T(8,128)(2,1)S(1)}, u32[]{:S(2)}, u32[]{:S(2)}) collective-permute-start(bf16[2,1,512,1,128]{4,2,3,1,0:T(8,128)(2,1)S(1)} %pad_maximum_fusion), channel_id=1, source_target_pairs={{0,64},{8,72},{16,80},{24,88},{32,96},{40,104},{48,112},{56,120},{... | collective-permute-start | bytes 786440 | tf_op jit(solution)/shard_map/ppermute | solution.py:11
  12.3 34.2 %collective-permute-start.2 = (bf16[2,1,512,1,128]{4,2,3,1,0:T(8,128)(2,1)S(1)}, bf16[2,1,512,1,128]{4,2,3,1,0:T(8,128)(2,1)S(1)}, u32[]{:S(2)}, u32[]{:S(2)}) collective-permute-start(bf16[2,1,512,1,128]{4,2,3,1,0:T(8,128)(2,1)S(1)} %pad_maximum_fusion), channel_id=1, source_target_pairs={{0,32},{8,40},{16,48},{24,56},{32,0},{40,8},{48,16},{56,24},{64,96... | collective-permute-start | bytes 786440 | tf_op jit(solution)/shard_map/ppermute | solution.py:11
  17.1 12.5 %collective-permute-start.1 = (bf16[2,1,512,1,128]{4,2,3,1,0:T(8,128)(2,1)S(1)}, bf16[2,1,512,1,128]{4,2,3,1,0:T(8,128)(2,1)S(1)}, u32[]{:S(2)}, u32[]{:S(2)}) collective-permute-start(bf16[2,1,512,1,128]{4,2,3,1,0:T(8,128)(2,1)S(1)} %pad_maximum_fusion), channel_id=1, source_target_pairs={{0,16},{8,24},{16,0},{24,8},{32,48},{40,56},{48,32},{56,40},{64,80... | collective-permute-start | bytes 786440 | tf_op jit(solution)/shard_map/ppermute | solution.py:11
  19.4 29.9 %collective-permute-start = (bf16[2,1,512,1,128]{4,2,3,1,0:T(8,128)(2,1)S(1)}, bf16[2,1,512,1,128]{4,2,3,1,0:T(8,128)(2,1)S(1)}, u32[]{:S(2)}, u32[]{:S(2)}) collective-permute-start(bf16[2,1,512,1,128]{4,2,3,1,0:T(8,128)(2,1)S(1)} %pad_maximum_fusion), channel_id=1, source_target_pairs={{0,8},{8,0},{16,24},{24,16},{32,40},{40,32},{48,56},{56,48},{64,72... | collective-permute-start | bytes 786440 | tf_op jit(solution)/shard_map/ppermute | solution.py:11
  22.9 27.9 %collective-permute-start.4 = (bf16[2,1,512,1,128]{4,2,3,1,0:T(8,128)(2,1)S(1)}, bf16[2,1,512,1,128]{4,2,3,1,0:T(8,128)(2,1)S(1)}, u32[]{:S(2)}, u32[]{:S(2)}) collective-permute-start(bf16[2,1,512,1,128]{4,2,3,1,0:T(8,128)(2,1)S(1)} %pad_maximum_fusion), channel_id=1, source_target_pairs={{0,128},{8,136},{16,144},{24,152},{32,160},{40,168},{48,176},{56,1... | collective-permute-start | bytes 786440 | tf_op jit(solution)/shard_map/ppermute | solution.py:11
  29.6 27.4 %collective-permute-start.5 = (bf16[2,1,512,1,128]{4,2,3,1,0:T(8,128)(2,1)S(1)}, bf16[2,1,512,1,128]{4,2,3,1,0:T(8,128)(2,1)S(1)}, u32[]{:S(2)}, u32[]{:S(2)}) collective-permute-start(bf16[2,1,512,1,128]{4,2,3,1,0:T(8,128)(2,1)S(1)} %pad_maximum_fusion), channel_id=1, source_target_pairs={{0,256},{8,264},{16,272},{24,280},{32,288},{40,296},{48,304},{56,3... | collective-permute-start | bytes 786440 | tf_op jit(solution)/shard_map/ppermute | solution.py:11
  52.2 6.2 %copy-start.1 = (bf16[512,128]{1,0:T(8,128)(2,1)S(1)}, bf16[512,128]{1,0:T(8,128)(2,1)}, u32[]{:S(2)}) copy-start(bf16[512,128]{1,0:T(8,128)(2,1)} %param.6) | copy-start | bytes 393220
Sparse Core Ops, SparseCore 0:
  11.9 153.8 all-gather.1
  172.5 93.8 reduce-scatter.1
where the time goes:
time: 274 us; the launch traced here: 273 us
  waiting for transfers between devices  199 us (73%)
  starting transfers between devices  34.3 us (13%)
  matrix products  20 us (7%)
  between operations  13.6 us (5%)
  other arithmetic  6 us (2%)
    all_gather x1, waiting for transfers between devices, shards(): lax.all_gather(out_weight, 'ctx', axis=1, tiled=True)  99.9 us
    reduce_scatter x1, waiting for transfers between devices, shards(): lax.psum_scatter(terms.astype(jnp.bfloat16), 'head', scatter_dimension=1,...  94 us
    ppermute x6, starting transfers between devices, from_partner(): lax.ppermute(shard, axis, [(i, i ^ 1 << bit) for i in range(lax.axis_size...  34.3 us
    dot_general x7, matrix products, block_stats(): jnp.einsum('bgrqk,bkgd->bgrqd', probs, pair[1], preferred_element_type=jn...  7.46 us
    dot_general x1, matrix products, shards(): jnp.dot(hidden, lax.all_gather(out_weight, 'ctx', axis=1, tiled=True), pr...  6.56 us
    dot_general x7, matrix products, block_stats(): jnp.einsum('bqgrd,bkgd->bgrqk', queries, pair[0], preferred_element_type=...  5.96 us
  transfers between devices with their start and end apart: 8, of which 3 were waited for; matrix products, arithmetic and copies ran while one was open for 7% of the time, Pallas kernels for 0%

commit v1 on v0

v1 whole, which is shorter than its diff:
```python
import math

import jax
import jax.numpy as jnp
from jax import lax
from jax.experimental import pallas as pl
from jax.experimental.pallas import tpu as pltpu
from jax.sharding import PartitionSpec as P

HD = 128
BLOCK = 512
GROUP = 4
NH = 8
SCALE = HD ** (-0.5) * math.log2(math.e)
MESH = pl.DeviceIdType.MESH
BF = jnp.bfloat16
F32 = jnp.float32


def flip(c, bit):
    return c + bit * (1 - 2 * lax.rem(lax.div(c, bit), 2))


def kernel(
    q_ref, k_ref, v_ref, w_ref, o_ref,
    qt, kb, vb, m_s, l_s, acc, ht, w1, wg, buf, og,
    k_send, k_recv, v_send, v_recv,
    wz_sem, w1a_send, w1a_recv, w1b_send, w1b_recv, w1c_send, w1c_recv,
    a2_send, a2_recv, wga_send, wga_recv, wgb_send, wgb_recv, wgc_send, wgc_recv,
    c_send, c_recv,
):
    c = lax.axis_index("ctx")
    p = lax.axis_index("head")
    zh = lax.div(c, 32)
    x = lax.rem(lax.div(c, 8), 4)
    y = lax.rem(lax.div(c, 2), 4)
    core = lax.rem(c, 2)
    partners = [None] + [flip(c, b) for b in (1, 2, 8, 4, 16, 32)]

    def at_x(r):
        nx = lax.rem(x + (r + 4), 4)
        return {"ctx": c + 8 * (nx - x)}, nx

    def at_y(r):
        ny = lax.rem(y + (r + 4), 4)
        return {"ctx": c + 2 * (ny - y)}, ny

    barrier = pltpu.get_barrier_semaphore()
    peers = [{"ctx": partners[1]}, {"ctx": partners[6]}]
    peers += [at_x(r)[0] for r in (1, 2, 3)] + [at_y(r)[0] for r in (1, 2, 3)]
    peers += [{"head": lax.rem(p + r, NH)} for r in range(1, NH)]
    for peer in peers:
        pl.semaphore_signal(barrier, inc=1, device_id=peer, device_id_type=MESH)

    def remote(src, dst, send, recv, peer):
        return pltpu.make_async_remote_copy(
            src_ref=src, dst_ref=dst, send_sem=send, recv_sem=recv,
            device_id=peer, device_id_type=MESH,
        )

    for g in range(GROUP):
        for tile in range(2):
            rows = q_ref[tile * 256:(tile + 1) * 256, g * HD:(g + 1) * HD]
            qt[tile * GROUP + g] = rows.T
    kb[0] = k_ref[...]
    vb[0] = v_ref[...].T
    own_w = 4 * zh + x
    w1[own_w, y, core] = w_ref[...]
    m_s[...] = jnp.full(m_s.shape, -1e30, F32)
    l_s[...] = jnp.zeros(l_s.shape, F32)
    acc[...] = jnp.zeros(acc.shape, F32)

    def attend(j, low, high):
        def one(i, carry):
            s = jnp.dot(kb[j], qt[i], preferred_element_type=F32)
            old = m_s[i]
            top = jnp.maximum(old, jnp.max(s, axis=0, keepdims=True))
            weights = jnp.exp2((s - top) * SCALE)
            fade = jnp.exp2((old - top) * SCALE)
            m_s[i] = top
            l_s[i] = fade * l_s[i] + jnp.sum(weights, axis=0, keepdims=True)
            part = jnp.dot(vb[j], weights.astype(BF), preferred_element_type=F32)
            acc[i] = fade * acc[i] + part
            return carry

        lax.fori_loop(low, high, one, 0)

    attend(0, 0, 8)
    pl.semaphore_wait(barrier, len(peers))

    other_w = 4 * (1 - zh) + x
    far = {"ctx": partners[6]}
    wz = remote(w1.at[own_w, y, core], w1.at[own_w, y, core], wz_sem.at[0], wz_sem.at[1], far)
    wz.start()

    def kv_copies(j, peer):
        return (
            remote(kb.at[0], kb.at[j], k_send.at[j - 1], k_recv.at[j - 1], peer),
            remote(vb.at[0], vb.at[j], v_send.at[j - 1], v_recv.at[j - 1], peer),
        )

    kv = [None]
    for j in range(1, 7):
        kv.append(kv_copies(j, {"ctx": partners[j]}))
    for j in (6, 1, 2, 3, 4, 5):
        for copy in kv[j]:
            copy.start()

    def kv_wait(j):
        for copy in kv_copies(j, far):
            copy.wait_recv()

    def near(j, carry):
        kv_wait(j)
        attend(j, 0, 8)
        return carry

    half = [pl.ds(0, 256), pl.ds(256, 256)]

    def w1_one(which, h, nx, ny):
        d = 4 * (zh if which == 0 else 1 - zh) + nx
        return w1.at[d, ny, core, :, half[h]]

    def w1_line(which, h, n):
        z = zh if which == 0 else 1 - zh
        if h == 0:
            return w1.at[4 * z + n, :, core, :, half[h]]
        return w1.at[pl.ds(4 * z, 4), n, core, :, half[h]]

    def w1_plane(which, h, co):
        z = zh if which == 0 else 1 - zh
        return w1.at[pl.ds(4 * z, 4), :, co, :, half[h]]

    def wg_one(h, nx, ny):
        return wg.at[:, nx, ny, core, :, half[h]]

    def wg_line(h, n):
        if h == 0:
            return wg.at[:, n, :, core, :, half[h]]
        return wg.at[:, :, n, core, :, half[h]]

    def wg_plane(h, co):
        return wg.at[:, :, :, co, :, half[h]]

    def phase_a(one, send, recv, h):
        first = at_y if h == 0 else at_x
        out, arrive = [], []
        for r in (1, 2, 3):
            peer, _ = first(r)
            block = one(h, x, y)
            out.append(remote(block, block, send.at[r - 1], recv.at[r - 1], peer))
            _, n = first(-r)
            block = one(h, x, n) if h == 0 else one(h, n, y)
            arrive.append(remote(block, block, send.at[r - 1], recv.at[r - 1], peer))
        return out, arrive

    def phase_b(line, send, recv, h):
        second = at_x if h == 0 else at_y
        out, arrive = [], []
        for r in (1, 2, 3):
            peer, _ = second(r)
            block = line(h, x if h == 0 else y)
            out.append(remote(block, block, send.at[r - 1], recv.at[r - 1], peer))
            _, n = second(-r)
            block = line(h, n)
            arrive.append(remote(block, block, send.at[r - 1], recv.at[r - 1], peer))
        return out, arrive

    def phase_c(plane, send, recv, h):
        peer = {"ctx": partners[1]}
        block = plane(h, core)
        out = [remote(block, block, send, recv, peer)]
        block = plane(h, 1 - core)
        arrive = [remote(block, block, send, recv, peer)]
        return out, arrive

    def start(pair):
        for copy in pair[0]:
            copy.start()

    def arrived(pair):
        for copy in pair[1]:
            copy.wait_recv()

    def sent(pair):
        for copy in pair[0]:
            copy.wait_send()

    w1a, w1b, w1c = {}, {}, {}
    for which in range(2):
        for h in range(2):
            key = (which, h)
            w1a[key] = phase_a(
                lambda hh, nx, ny, which=which: w1_one(which, hh, nx, ny),
                w1a_send.at[which, h], w1a_recv.at[which, h], h)
            w1b[key] = phase_b(
                lambda hh, n, which=which: w1_line(which, hh, n),
                w1b_send.at[which, h], w1b_recv.at[which, h], h)
            w1c[key] = phase_c(
                lambda hh, co, which=which: w1_plane(which, hh, co),
                w1c_send.at[which, h], w1c_recv.at[which, h], h)
    wga = [phase_a(wg_one, wga_send.at[h], wga_recv.at[h], h) for h in range(2)]
    wgb = [phase_b(wg_line, wgb_send.at[h], wgb_recv.at[h], h) for h in range(2)]
    wgc = [phase_c(wg_plane, wgc_send.at[h], wgc_recv.at[h], h) for h in range(2)]

    for h in range(2):
        start(w1a[0, h])
    lax.fori_loop(1, 4, near, 0)
    for h in range(2):
        arrived(w1a[0, h])
        start(w1b[0, h])
    remote(w1.at[other_w, y, core], w1.at[other_w, y, core], wz_sem.at[0], wz_sem.at[1], far).wait_recv()
    for h in range(2):
        start(w1a[1, h])
    lax.fori_loop(4, 6, near, 0)
    for h in range(2):
        arrived(w1a[1, h])
        start(w1b[1, h])
    for h in range(2):
        arrived(w1b[0, h])
        start(w1c[0, h])
    for h in range(2):
        arrived(w1b[1, h])
        start(w1c[1, h])

    right = {"head": lax.rem(p + 1, NH)}
    left = {"head": lax.rem(p + NH - 1, NH)}

    def chain(way, k, q, src):
        return remote(src, buf.at[way, k, q], c_send.at[way, k, q], c_recv.at[way, k, q],
                      right if way == 0 else left)

    has_up = (p > 0, p < NH - 1)
    has_down = (p < NH - 1, p > 0)
    place = (p, NH - 1 - p)

    def finish(tile):
        for g in range(GROUP):
            i = tile * GROUP + g
            value = (acc[i] / l_s[i]).astype(BF)
            for q in range(2):
                ht[tile * 2 + q, g * HD:(g + 1) * HD, :] = value[:, q * 128:(q + 1) * 128]

    kv_wait(6)
    attend(6, 0, 4)
    finish(0)
    for q in range(2):
        for way in range(2):
            @pl.when(has_down[way])
            def _():
                chain(way, 0, q, ht.at[q]).start()
    attend(6, 4, 8)
    finish(1)
    for which in range(2):
        for h in range(2):
            arrived(w1c[which, h])

    u = x * 8 + y * 2 + core
    uy, uc, uo = lax.div(u, 8), lax.rem(lax.div(u, 4), 2), lax.rem(u, 4) * 16
    wg[p, x, y, core] = w1[p, uy, uc, pl.ds(pl.multiple_of(uo, 16), 16)]

    def a2(r):
        d = lax.rem(p + r, NH)
        return remote(
            w1.at[d, uy, uc, pl.ds(pl.multiple_of(uo, 16), 16)], wg.at[p, x, y, core],
            a2_send.at[r - 1], a2_recv.at[r - 1], {"head": d})

    for r in range(1, NH):
        a2(r).start()

    def term(d, q):
        return jnp.dot(w1[d].reshape(512, 512), ht[2 + q], preferred_element_type=F32)

    def step(k, carry):
        for q in range(2):
            for way in range(2):
                slot = buf.at[way, k - 1, q]

                @pl.when(has_up[way])
                def _():
                    chain(way, k - 1, q, slot).wait_recv()

                adds = jnp.logical_and(k > place[way], has_down[way])
                far_place = NH + place[way] - k
                d = far_place if way == 0 else NH - 1 - far_place

                @pl.when(jnp.logical_and(adds, has_up[way]))
                def _():
                    slot[...] = (slot[...].astype(F32) + term(d, q)).astype(BF)

                @pl.when(jnp.logical_and(adds, jnp.logical_not(has_up[way])))
                def _():
                    slot[...] = term(d, q).astype(BF)

                @pl.when(has_down[way])
                def _():
                    chain(way, k - 1, q, slot).wait_send()
                    chain(way, k, q, slot).start()
        return carry

    lax.fori_loop(1, 3, step, 0)
    for r in range(1, NH):
        h = lax.rem(p + (NH - r), NH)
        block = wg.at[h, x, y, core]
        remote(block, block, a2_send.at[r - 1], a2_recv.at[r - 1], right).wait_recv()
    for h in range(2):
        start(wga[h])
    lax.fori_loop(3, 4, step, 0)
    for h in range(2):
        arrived(wga[h])
        start(wgb[h])
    lax.fori_loop(4, 6, step, 0)
    for h in range(2):
        arrived(wgb[h])
        start(wgc[h])
    lax.fori_loop(6, 8, step, 0)

    for h in range(2):
        arrived(wgc[h])
    for q in range(2):
        og[q] = jnp.dot(wg[p].reshape(512, 512), ht[q], preferred_element_type=F32)

    def gathered(h, carry):
        for q in range(2):
            @pl.when(h < p)
            def _():
                og[q] += jnp.dot(wg[h].reshape(512, 512), buf[0, p - 1 - h, q], preferred_element_type=F32)

            @pl.when(h > p)
            def _():
                og[q] += jnp.dot(wg[h].reshape(512, 512), buf[1, h - p - 1, q], preferred_element_type=F32)
        return carry

    lax.fori_loop(0, NH, gathered, 0)
    for q in range(2):
        o_ref[q * 128:(q + 1) * 128, :] = og[q].T.astype(BF)
    for q in range(2):
        og[q] = term(p, q)
    for q in range(2):
        for way in range(2):
            @pl.when(has_up[way])
            def _():
                chain(way, NH - 1, q, ht.at[q]).wait_recv()
                og[q] += buf[way, NH - 1, q].astype(F32)
        o_ref[256 + q * 128:256 + (q + 1) * 128, :] = og[q].T.astype(BF)

    for q in range(2):
        for way in range(2):
            @pl.when(has_down[way])
            def _():
                chain(way, NH - 1, q, ht.at[q]).wait_send()
    wz.wait_send()
    for j in range(1, 7):
        for copy in kv[j]:
            copy.wait_send()
    for which in range(2):
        for h in range(2):
            sent(w1a[which, h])
            sent(w1b[which, h])
            sent(w1c[which, h])
    for r in range(1, NH):
        a2(r).wait_send()
    for h in range(2):
        sent(wga[h])
        sent(wgb[h])
        sent(wgc[h])


def shards(query_rows, key_rows, value_rows, out_weight):
    dma = pltpu.SemaphoreType.DMA
    vmem = pl.BlockSpec(memory_space=pltpu.VMEM)
    return pl.pallas_call(
        kernel,
        out_shape=jax.ShapeDtypeStruct((BLOCK, GROUP * HD), BF),
        in_specs=[vmem] * 4,
        out_specs=vmem,
        scratch_shapes=[
            pltpu.VMEM((8, HD, 256), BF),
            pltpu.VMEM((7, BLOCK, HD), BF),
            pltpu.VMEM((7, HD, BLOCK), BF),
            pltpu.VMEM((8, 1, 256), F32),
            pltpu.VMEM((8, 1, 256), F32),
            pltpu.VMEM((8, HD, 256), F32),
            pltpu.VMEM((4, 512, 128), BF),
            pltpu.VMEM((8, 4, 2, 64, 512), BF),
            pltpu.VMEM((8, 4, 4, 2, 16, 512), BF),
            pltpu.VMEM((2, 8, 2, 512, 128), BF),
            pltpu.VMEM((2, 512, 128), F32),
            dma((6,)), dma((6,)), dma((6,)), dma((6,)),
            dma((2,)),
            dma((2, 2, 3)), dma((2, 2, 3)), dma((2, 2, 3)), dma((2, 2, 3)), dma((2, 2)), dma((2, 2)),
            dma((7,)), dma((7,)),
            dma((2, 3)), dma((2, 3)), dma((2, 3)), dma((2, 3)), dma((2,)), dma((2,)),
            dma((2, 8, 2)), dma((2, 8, 2)),
        ],
        compiler_params=pltpu.CompilerParams(
            collective_id=0, has_side_effects=True, vmem_limit_bytes=48 * 1024 * 1024
        ),
        cost_estimate=pl.CostEstimate(flops=6_000_000_000, bytes_accessed=2_000_000, transcendentals=7_400_000),
    )(query_rows, key_rows, value_rows, out_weight.T)


def solution(mesh):
    placed = (P("ctx", "head"), P("ctx", "head"), P("ctx", "head"), P("head", "ctx"))
    return jax.shard_map(
        shards, mesh=mesh, in_specs=placed, out_specs=P("ctx", "head"), check_vma=False
    )
```

time: 274 us -> 108 us (0.39)
  the two profiles are of different devices: /device:TPU:1 before, /device:TPU:52 now
where the time goes in v1:
time: 108 us
  Pallas kernels  103 us (95%)
  local copies, waits for them, and re-layouts  4.48 us (4%)
    pallas_call x1, Pallas kernels, shards(): pl.pallas_call(kernel, out_shape=jax.ShapeDtypeStruct((BLOCK, GROUP * HD)...  103 us
    unnamed x9, local copies, waits for them, and re-layouts  4.48 us

profile of v1, /device:TPU:52, one launch (start us, length us, event | category | flops | bytes accessed | tf_op | source)
XLA Modules:
  0.0 107.6 jit_solution(2178246765312455919)
XLA Ops:
  0.0 0.0 copy-start
  0.0 1.0 copy-done
  1.0 0.0 copy-start.1
  1.0 0.9 copy-done.1
  1.9 0.0 copy-start.2
  1.9 0.9 copy-done.2
  2.9 0.0 copy-start.3
  2.9 0.8 copy-done.3
  3.7 103.1 %shard_map.46 = bf16[512,512]{1,0:T(8,128)(2,1)S(1)} custom-call(bf16[512,512]{1,0:T(8,128)(2,1)S(1)} %copy-done, bf16[512,128]{1,0:T(8,128)(2,1)S(1)} %copy-done.1, bf16[512,128]{1,0:T(8,128)(2,1)S(1)} %copy-done.2, bf16[64,512]{1,0:T(8,128)(2,1)S(1)} %bitcast.1), custom_call_target="tpu_custom_call" | custom-call | flops 6000000000 | bytes 2000000 | tf_op jit(solution)/shard_map/pallas_call | solution.py:372
  106.8 0.8 copy.6
Async XLA Ops:
  0.0 1.0 copy-start
  1.0 0.9 copy-start.1
  1.9 0.9 copy-start.2
  2.9 0.8 copy-start.3

commit v2 on v1

--- a/solution.py
+++ b/solution.py
@@ -22,8 +22,8 @@
 
 
 def kernel(
-    q_ref, k_ref, v_ref, w_ref, o_ref,
-    qt, kb, vb, m_s, l_s, acc, ht, w1, wg, buf, og,
+    q_hbm, k_hbm, v_hbm, w_hbm, o_ref,
+    q_ref, v_ref, qt, kb, vb, m_s, l_s, acc, ht, w1, wg, buf, og, in_sem,
     k_send, k_recv, v_send, v_recv,
     wz_sem, w1a_send, w1a_recv, w1b_send, w1b_recv, w1c_send, w1c_recv,
     a2_send, a2_recv, wga_send, wga_recv, wgb_send, wgb_recv, wgc_send, wgc_recv,
@@ -48,7 +48,13 @@
     barrier = pltpu.get_barrier_semaphore()
     peers = [{"ctx": partners[1]}, {"ctx": partners[6]}]
     peers += [at_x(r)[0] for r in (1, 2, 3)] + [at_y(r)[0] for r in (1, 2, 3)]
-    peers += [{"head": lax.rem(p + r, NH)} for r in range(1, NH)]
+    ring = (1, 2, 3, 4, -1, -2, -3)
+
+    def at_z(r):
+        z = lax.rem(8 * zh + p + (r + 16), 16)
+        return {"ctx": c + 32 * (lax.div(z, 8) - zh), "head": lax.rem(z, 8)}, lax.rem(z, 8)
+
+    peers += [at_z(-r)[0] for r in ring]
     for peer in peers:
         pl.semaphore_signal(barrier, inc=1, device_id=peer, device_id_type=MESH)
 
@@ -58,34 +64,47 @@
             device_id=peer, device_id_type=MESH,
         )
 
+    own_w = 4 * zh + x
+    loads = [
+        pltpu.make_async_copy(v_hbm, v_ref, in_sem.at[0]),
+        pltpu.make_async_copy(k_hbm, kb.at[0], in_sem.at[1]),
+        pltpu.make_async_copy(q_hbm, q_ref, in_sem.at[2]),
+        pltpu.make_async_copy(w_hbm, w1.at[own_w, y, core], in_sem.at[3]),
+    ]
+    for copy in loads:
+        copy.start()
+    m_s[...] = jnp.full(m_s.shape, -1e30, F32)
+    l_s[...] = jnp.zeros(l_s.shape, F32)
+    acc[...] = jnp.zeros(acc.shape, F32)
+    loads[0].wait()
+    vb[0] = v_ref[...].T
+    loads[1].wait()
+    loads[2].wait()
     for g in range(GROUP):
         for tile in range(2):
             rows = q_ref[tile * 256:(tile + 1) * 256, g * HD:(g + 1) * HD]
             qt[tile * GROUP + g] = rows.T
-    kb[0] = k_ref[...]
-    vb[0] = v_ref[...].T
-    own_w = 4 * zh + x
-    w1[own_w, y, core] = w_ref[...]
-    m_s[...] = jnp.full(m_s.shape, -1e30, F32)
-    l_s[...] = jnp.zeros(l_s.shape, F32)
-    acc[...] = jnp.zeros(acc.shape, F32)
-
-    def attend(j, low, high):
-        def one(i, carry):
-            s = jnp.dot(kb[j], qt[i], preferred_element_type=F32)
-            old = m_s[i]
-            top = jnp.maximum(old, jnp.max(s, axis=0, keepdims=True))
-            weights = jnp.exp2((s - top) * SCALE)
-            fade = jnp.exp2((old - top) * SCALE)
-            m_s[i] = top
-            l_s[i] = fade * l_s[i] + jnp.sum(weights, axis=0, keepdims=True)
-            part = jnp.dot(vb[j], weights.astype(BF), preferred_element_type=F32)
-            acc[i] = fade * acc[i] + part
-            return carry
-
-        lax.fori_loop(low, high, one, 0)
-
-    attend(0, 0, 8)
+    loads[3].wait()
+
+    def attend(j, tile):
+        part = range(tile * GROUP, (tile + 1) * GROUP)
+        scores = [jnp.dot(kb[j], qt[i], preferred_element_type=F32) for i in part]
+        old = [m_s[i] for i in part]
+        top = [jnp.maximum(o, jnp.max(s, axis=0, keepdims=True)) for o, s in zip(old, scores)]
+        weights = [jnp.exp2((s - t) * SCALE) for s, t in zip(scores, top)]
+        fade = [jnp.exp2((o - t) * SCALE) for o, t in zip(old, top)]
+        total = [f * l_s[i] + jnp.sum(w, axis=0, keepdims=True) for f, i, w in zip(fade, part, weights)]
+        output = [
+            f * acc[i] + jnp.dot(vb[j], w.astype(BF), preferred_element_type=F32)
+            for f, i, w in zip(fade, part, weights)
+        ]
+        for n, i in enumerate(part):
+            m_s[i] = top[n]
+            l_s[i] = total[n]
+            acc[i] = output[n]
+
+    attend(0, 0)
+    attend(0, 1)
     pl.semaphore_wait(barrier, len(peers))
 
     other_w = 4 * (1 - zh) + x
@@ -102,7 +121,7 @@
     kv = [None]
     for j in range(1, 7):
         kv.append(kv_copies(j, {"ctx": partners[j]}))
-    for j in (6, 1, 2, 3, 4, 5):
+    for j in (6, 1):
         for copy in kv[j]:
             copy.start()
 
@@ -112,7 +131,8 @@
 
     def near(j, carry):
         kv_wait(j)
-        attend(j, 0, 8)
+        attend(j, 0)
+        attend(j, 1)
         return carry
 
     half = [pl.ds(0, 256), pl.ds(256, 256)]
@@ -205,17 +225,21 @@
 
     for h in range(2):
         start(w1a[0, h])
-    lax.fori_loop(1, 4, near, 0)
+    for j in range(2, 6):
+        for copy in kv[j]:
+            copy.start()
+    lax.fori_loop(1, 2, near, 0)
     for h in range(2):
         arrived(w1a[0, h])
         start(w1b[0, h])
     remote(w1.at[other_w, y, core], w1.at[other_w, y, core], wz_sem.at[0], wz_sem.at[1], far).wait_recv()
     for h in range(2):
         start(w1a[1, h])
-    lax.fori_loop(4, 6, near, 0)
+    lax.fori_loop(2, 3, near, 0)
     for h in range(2):
         arrived(w1a[1, h])
         start(w1b[1, h])
+    lax.fori_loop(3, 6, near, 0)
     for h in range(2):
         arrived(w1b[0, h])
         start(w1c[0, h])
@@ -241,32 +265,32 @@
             for q in range(2):
                 ht[tile * 2 + q, g * HD:(g + 1) * HD, :] = value[:, q * 128:(q + 1) * 128]
 
+    for which in range(2):
+        for h in range(2):
+            arrived(w1c[which, h])
+    u = x * 8 + y * 2 + core
+    uy, uc, uo = lax.div(u, 8), lax.rem(lax.div(u, 4), 2), lax.rem(u, 4) * 16
+    wg[p, x, y, core] = w1[p, uy, uc, pl.ds(pl.multiple_of(uo, 16), 16)]
+
+    def a2(n):
+        peer, d = at_z(ring[n])
+        return remote(
+            w1.at[d, uy, uc, pl.ds(pl.multiple_of(uo, 16), 16)], wg.at[p, x, y, core],
+            a2_send.at[n], a2_recv.at[n], peer)
+
+    for n in range(len(ring)):
+        a2(n).start()
+
     kv_wait(6)
-    attend(6, 0, 4)
+    attend(6, 0)
     finish(0)
     for q in range(2):
         for way in range(2):
             @pl.when(has_down[way])
             def _():
                 chain(way, 0, q, ht.at[q]).start()
-    attend(6, 4, 8)
+    attend(6, 1)
     finish(1)
-    for which in range(2):
-        for h in range(2):
-            arrived(w1c[which, h])
-
-    u = x * 8 + y * 2 + core
-    uy, uc, uo = lax.div(u, 8), lax.rem(lax.div(u, 4), 2), lax.rem(u, 4) * 16
-    wg[p, x, y, core] = w1[p, uy, uc, pl.ds(pl.multiple_of(uo, 16), 16)]
-
-    def a2(r):
-        d = lax.rem(p + r, NH)
-        return remote(
-            w1.at[d, uy, uc, pl.ds(pl.multiple_of(uo, 16), 16)], wg.at[p, x, y, core],
-            a2_send.at[r - 1], a2_recv.at[r - 1], {"head": d})
-
-    for r in range(1, NH):
-        a2(r).start()
 
     def term(d, q):
         return jnp.dot(w1[d].reshape(512, 512), ht[2 + q], preferred_element_type=F32)
@@ -299,10 +323,9 @@
         return carry
 
     lax.fori_loop(1, 3, step, 0)
-    for r in range(1, NH):
-        h = lax.rem(p + (NH - r), NH)
-        block = wg.at[h, x, y, core]
-        remote(block, block, a2_send.at[r - 1], a2_recv.at[r - 1], right).wait_recv()
+    for n in range(len(ring)):
+        block = wg.at[at_z(-ring[n])[1], x, y, core]
+        remote(block, block, a2_send.at[n], a2_recv.at[n], right).wait_recv()
     for h in range(2):
         start(wga[h])
     lax.fori_loop(3, 4, step, 0)
@@ -358,8 +381,8 @@
             sent(w1a[which, h])
             sent(w1b[which, h])
             sent(w1c[which, h])
-    for r in range(1, NH):
-        a2(r).wait_send()
+    for n in range(len(ring)):
+        a2(n).wait_send()
     for h in range(2):
         sent(wga[h])
         sent(wgb[h])
@@ -372,9 +395,11 @@
     return pl.pallas_call(
         kernel,
         out_shape=jax.ShapeDtypeStruct((BLOCK, GROUP * HD), BF),
-        in_specs=[vmem] * 4,
+        in_specs=[pl.BlockSpec(memory_space=pltpu.HBM)] * 4,
         out_specs=vmem,
         scratch_shapes=[
+            pltpu.VMEM((BLOCK, GROUP * HD), BF),
+            pltpu.VMEM((BLOCK, HD), BF),
             pltpu.VMEM((8, HD, 256), BF),
             pltpu.VMEM((7, BLOCK, HD), BF),
             pltpu.VMEM((7, HD, BLOCK), BF),
@@ -386,6 +411,7 @@
             pltpu.VMEM((8, 4, 4, 2, 16, 512), BF),
             pltpu.VMEM((2, 8, 2, 512, 128), BF),
             pltpu.VMEM((2, 512, 128), F32),
+            dma((4,)),
             dma((6,)), dma((6,)), dma((6,)), dma((6,)),
             dma((2,)),
             dma((2, 2, 3)), dma((2, 2, 3)), dma((2, 2, 3)), dma((2, 2, 3)), dma((2, 2)), dma((2, 2)),
@@ -394,7 +420,7 @@
             dma((2, 8, 2)), dma((2, 8, 2)),
         ],
         compiler_params=pltpu.CompilerParams(
-            collective_id=0, has_side_effects=True, vmem_limit_bytes=48 * 1024 * 1024
+            collective_id=0, has_side_effects=True, vmem_limit_bytes=60 * 1024 * 1024
         ),
         cost_estimate=pl.CostEstimate(flops=6_000_000_000, bytes_accessed=2_000_000, transcendentals=7_400_000),
     )(query_rows, key_rows, value_rows, out_weight.T)

time: 108 us -> 104 us (0.963)
  the two profiles are of different devices: /device:TPU:52 before, /device:TPU:1 now
where the time goes in v2:
time: 104 us; the launch traced here: 103 us
  Pallas kernels  101 us (97%)
  local copies, waits for them, and re-layouts  1.87 us (2%)
    pallas_call x1, Pallas kernels, shards(): pl.pallas_call(kernel, out_shape=jax.ShapeDtypeStruct((BLOCK, GROUP * HD)...  101 us

profile of v2, /device:TPU:1, one launch (start us, length us, event | category | flops | bytes accessed | tf_op | source)
XLA Modules:
  0.0 103.4 jit_solution(14421935854070744075)
XLA Ops:
  0.0 101.5 %shard_map.46 = bf16[512,512]{1,0:T(8,128)(2,1)} custom-call(bf16[512,512]{1,0:T(8,128)(2,1)} %q_hbm.1, bf16[512,128]{1,0:T(8,128)(2,1)} %k_hbm.1, bf16[512,128]{1,0:T(8,128)(2,1)} %v_hbm.1, bf16[64,512]{1,0:T(8,128)(2,1)} %bitcast.1), custom_call_target="tpu_custom_call" | custom-call | flops 6000000000 | bytes 2000000 | tf_op jit(solution)/shard_map/pallas_call | solution.py:395
  101.5 1.9 %copy.6 = bf16[512,512]{1,0:T(8,128)(2,1)} copy(bf16[512,512]{1,0:T(8,128)(2,1)} %shard_map.46) | data formatting | bytes 1048576

commit v3 on v2

--- a/solution.py
+++ b/solution.py
@@ -239,10 +239,11 @@
     for h in range(2):
         arrived(w1a[1, h])
         start(w1b[1, h])
-    lax.fori_loop(3, 6, near, 0)
+    lax.fori_loop(3, 5, near, 0)
     for h in range(2):
         arrived(w1b[0, h])
         start(w1c[0, h])
+    lax.fori_loop(5, 6, near, 0)
     for h in range(2):
         arrived(w1b[1, h])
         start(w1c[1, h])
@@ -318,7 +319,6 @@
 
                 @pl.when(has_down[way])
                 def _():
-                    chain(way, k - 1, q, slot).wait_send()
                     chain(way, k, q, slot).start()
         return carry
 
@@ -371,7 +371,8 @@
         for way in range(2):
             @pl.when(has_down[way])
             def _():
-                chain(way, NH - 1, q, ht.at[q]).wait_send()
+                for k in range(NH):
+                    chain(way, k, q, ht.at[q]).wait_send()
     wz.wait_send()
     for j in range(1, 7):
         for copy in kv[j]:

time: 104 us -> 104 us (level)
  no operation moved by 1% of the time
where the time goes in v3:
time: 104 us
  Pallas kernels  102 us (98%)
  local copies, waits for them, and re-layouts  1.87 us (2%)
    pallas_call x1, Pallas kernels, shards(): pl.pallas_call(kernel, out_shape=jax.ShapeDtypeStruct((BLOCK, GROUP * HD)...  102 us

profile of v3, /device:TPU:1, one launch (start us, length us, event | category | flops | bytes accessed | tf_op | source)
XLA Modules:
  0.0 103.6 jit_solution(12764838127829226020)
XLA Ops:
  0.0 101.7 %shard_map.46 = bf16[512,512]{1,0:T(8,128)(2,1)} custom-call(bf16[512,512]{1,0:T(8,128)(2,1)} %q_hbm.1, bf16[512,128]{1,0:T(8,128)(2,1)} %k_hbm.1, bf16[512,128]{1,0:T(8,128)(2,1)} %v_hbm.1, bf16[64,512]{1,0:T(8,128)(2,1)} %bitcast.1), custom_call_target="tpu_custom_call" | custom-call | flops 6000000000 | bytes 2000000 | tf_op jit(solution)/shard_map/pallas_call | solution.py:396
  101.8 1.9 %copy.6 = bf16[512,512]{1,0:T(8,128)(2,1)} copy(bf16[512,512]{1,0:T(8,128)(2,1)} %shard_map.46) | data formatting | bytes 1048576
